TPU v7x, 512 devices: a whole 4x8x8 slice. The times are simulated.
512 devices in a mesh: expert: 8 (over x, y_hi), dp: 64 (over z, y_lo, core).
Axes of the slice: x: 4, y: 8 (y_hi: 2, y_lo: 4; y = y_hi * 4 + y_lo), z: 8, core: 2. Of those that a mesh axis runs over, the one named last changes fastest.
Arguments:
- tokens: bfloat16 [64, 16, 2048], P('dp', 'expert'), may hold values from -6 to 6
- out_grad: bfloat16 [64, 16, 2048], P('dp', 'expert'), may hold values from -6 to 6
- expert_ids: int32 [64, 16, 2], P('dp'), may hold values from 0 to 7, as said below
- gate_scores: bfloat16 [64, 16, 2], P('dp'), may hold values from 0.25 to 1
- w_gate: bfloat16 [8, 2048, 8192], P('expert', None, 'dp'), may hold values from -0.125 to 0.125
- w_up: bfloat16 [8, 2048, 8192], P('expert', None, 'dp'), may hold values from -0.125 to 0.125
- w_down: bfloat16 [8, 8192, 2048], P('expert', 'dp'), may hold values from -0.0625 to 0.0625
Outputs:
- token_grad: bfloat16 [64, 16, 2048], P('dp', 'expert')
- grad_gate: bfloat16 [8, 2048, 8192], P('expert', None, 'dp')
- grad_up: bfloat16 [8, 2048, 8192], P('expert', None, 'dp')
- grad_down: bfloat16 [8, 8192, 2048], P('expert', 'dp')
Inputs may be any that keep to these rules, and one draw needn't show every extreme that they name: `expert_ids`: each token names two different experts; within a group no expert is named by more than 7 tokens, and in every group some expert is named by exactly 7 tokens.
All inputs are finite; a program needn't handle non-finite values.
Results may differ from a plain program's by a relative error of at most 0.0058.
Values may be sent and summed in bfloat16 or wider, within the bound.
A program may use at most 64 MiB of HBM per device.

v0:
```python
import jax
import jax.numpy as jnp
from jax import lax
from jax.sharding import PartitionSpec as P


def slot_table(expert_ids, experts):
    expert_range = jnp.arange(experts, dtype=jnp.int32)
    naming = jnp.sum((expert_ids[..., :, None] == expert_range).astype(jnp.int32), axis=-2)
    before = jnp.cumsum(naming, axis=-2) - naming
    return jnp.take_along_axis(before, expert_ids, axis=-1)


def local(tokens, out_grad, expert_ids, gate_scores, w_gate, w_up, w_down):
    tok_dev = tokens.shape[1]
    group_tok = expert_ids.shape[1]
    capacity = min(2 * tok_dev + 3, group_tok)
    experts = lax.axis_size("expert")
    my_expert = lax.axis_index("expert")
    group_ids = expert_ids[0]
    group_slots = slot_table(group_ids, experts)
    group_x, group_dy = (
        lax.all_gather(tokens, "expert", axis=1, tiled=True),
        lax.all_gather(out_grad, "expert", axis=1, tiled=True),
    )
    slot_range = jnp.arange(capacity, dtype=jnp.int32)
    matches = (group_ids[None, :, :] == my_expert) & (
        group_slots[None, :, :] == slot_range[:, None, None]
    )
    placing = jnp.sum(matches.astype(jnp.float32), axis=-1)
    weighting = jnp.sum(
        matches.astype(jnp.float32) * gate_scores[0].astype(jnp.float32)[None, :, :], axis=-1
    )
    x_picked = jnp.dot(
        placing.astype(jnp.bfloat16), group_x[0], preferred_element_type=jnp.float32
    ).astype(jnp.bfloat16)
    dy_picked = jnp.dot(
        weighting.astype(jnp.bfloat16), group_dy[0], preferred_element_type=jnp.float32
    ).astype(jnp.bfloat16)
    gate_slab = w_gate[0]
    up_slab = w_up[0]
    down_slab = w_down[0]
    input_rows = lax.all_gather(x_picked, "dp", axis=0, tiled=True)
    pre_gate = jnp.dot(input_rows, gate_slab, preferred_element_type=jnp.float32)
    pre_up = jnp.dot(input_rows, up_slab, preferred_element_type=jnp.float32)
    sigmoid_gate = jax.nn.sigmoid(pre_gate)
    activated = pre_gate * sigmoid_gate
    hidden = (activated * pre_up).astype(jnp.bfloat16)
    grad_rows = lax.all_gather(dy_picked, "dp", axis=0, tiled=True)
    grad_down = jnp.dot(hidden.T, grad_rows, preferred_element_type=jnp.float32).astype(
        jnp.bfloat16
    )
    grad_hidden = jnp.dot(grad_rows, down_slab.T, preferred_element_type=jnp.float32)
    gate_delta = (
        grad_hidden * pre_up * sigmoid_gate * (1.0 + pre_gate * (1.0 - sigmoid_gate))
    ).astype(jnp.bfloat16)
    up_delta = (grad_hidden * activated).astype(jnp.bfloat16)
    grad_gate = jnp.dot(input_rows.T, gate_delta, preferred_element_type=jnp.float32).astype(
        jnp.bfloat16
    )
    grad_up = jnp.dot(input_rows.T, up_delta, preferred_element_type=jnp.float32).astype(
        jnp.bfloat16
    )
    total = jnp.dot(gate_delta, gate_slab.T, preferred_element_type=jnp.float32)
    row_grad = lax.psum_scatter(
        total + jnp.dot(up_delta, up_slab.T, preferred_element_type=jnp.float32),
        "dp",
        scatter_dimension=0,
        tiled=True,
    )
    partial_tokens = jnp.dot(
        placing.T, row_grad, precision=lax.Precision.HIGHEST, preferred_element_type=jnp.float32
    )
    token_grad = lax.psum_scatter(partial_tokens, "expert", scatter_dimension=0, tiled=True)
    return (token_grad.astype(jnp.bfloat16)[None], grad_gate[None], grad_up[None], grad_down[None])


def solution(mesh):
    return jax.shard_map(
        local,
        mesh=mesh,
        in_specs=(
            P("dp", "expert", None),
            P("dp", "expert", None),
            P("dp", None, None),
            P("dp", None, None),
            P("expert", None, "dp"),
            P("expert", None, "dp"),
            P("expert", "dp", None),
        ),
        out_specs=(
            P("dp", "expert", None),
            P("expert", None, "dp"),
            P("expert", None, "dp"),
            P("expert", "dp", None),
        ),
        check_vma=False,
    )
```

profile of v0, /device:TPU:1, one launch (start us, length us, event | category | flops | bytes accessed | tf_op | source)
XLA Modules:
  0.0 555.3 jit_solution(10592391072857889739)
XLA Ops:
  11.2 38.7 %all_gather.14 = bf16[1,16,2048]{2,0,1:T(2,128)(2,1)S(1)} all-gather(bf16[1,2,2048]{2,0,1:T(2,128)(2,1)S(1)} %copy.75), channel_id=1, replica_groups=mesh['expert'=8,'dp'=64] {'expert'}, dimensions={1}, use_global_device_ids=true | all-gather | bytes 73728 | tf_op jit(solution)/shard_map/all_gather | solution.py:23
  50.8 37.7 %all_gather.12 = bf16[1,16,2048]{2,0,1:T(2,128)(2,1)S(1)} all-gather(bf16[1,2,2048]{2,0,1:T(2,128)(2,1)S(1)} %copy.74), channel_id=1, replica_groups=mesh['expert'=8,'dp'=64] {'expert'}, dimensions={1}, use_global_device_ids=true | all-gather | bytes 73728 | tf_op jit(solution)/shard_map/all_gather | solution.py:24
  88.5 0.8 fusion.4
  89.3 1.3 dynamic-slice.6
  90.6 1.3 dynamic-slice.2
  93.2 85.8 %all-gather.7.cloned.1.call-done = bf16[64,7,2048]{2,1,0:T(8,128)(2,1)} async-done(((bf16[1,7,2048]{2,1,0:T(8,128)(2,1)}), bf16[64,7,2048]{2,1,0:T(8,128)(2,1)}) %all-gather.7.cloned.1.call-update) | async-done | bytes 1835024 | tf_op jit(solution)/shard_map/all_gather | solution.py:43
  179.0 2.6 reshape.57
  183.3 114.6 %all-gather.5.cloned.1.call-done = bf16[64,7,2048]{2,1,0:T(8,128)(2,1)} async-done(((bf16[1,7,2048]{2,1,0:T(8,128)(2,1)}), bf16[64,7,2048]{2,1,0:T(8,128)(2,1)}) %all-gather.5.cloned.1.call-update) | async-done | bytes 1835024 | tf_op jit(solution)/shard_map/all_gather | solution.py:49
  297.8 3.7 reshape.55
  301.6 2.9 fusion.3
  305.8 2.4 convolution_add_fusion
  308.3 159.4 %fusion = f32[8,2048]{1,0:T(8,128)S(1)} fusion(f32[448,2048]{1,0:T(8,128)} %convolution_add_fusion), kind=kCustom, calls=%all-reduce-scatter | all-reduce-scatter fusion | flops 1048577 | bytes 3737600
  467.7 1.4 collective-permute-start.6
  469.1 1.3 collective-permute-start.5
  470.4 1.3 collective-permute-start.7
  471.7 1.6 fusion.2
  473.3 1.3 collective-permute-start.4
  474.6 13.6 %collective-permute-start.3 = (f32[8,2048]{1,0:T(8,128)S(1)}, f32[8,2048]{1,0:T(8,128)S(1)}, u32[]{:S(2)}, u32[]{:S(2)}) collective-permute-start(f32[8,2048]{1,0:T(8,128)S(1)} %fusion), channel_id=1, source_target_pairs={{0,4},{1,5},{2,6},{3,7},{4,8},{5,9},{6,10},{7,11},{8,12},{9,13},{1... | collective-permute-start | bytes 196616
  488.2 1.3 collective-permute-start.2
  489.5 6.6 %collective-permute-start.1 = (f32[8,2048]{1,0:T(8,128)S(1)}, f32[8,2048]{1,0:T(8,128)S(1)}, u32[]{:S(2)}, u32[]{:S(2)}) collective-permute-start(f32[8,2048]{1,0:T(8,128)S(1)} %fusion), channel_id=1, source_target_pairs={{0,2},{1,3},{2,4},{3,5},{4,6},{5,7},{6,8},{7,9},{8,10},{9,11},{10,... | collective-permute-start | bytes 196616
  496.1 2.5 collective-permute-start
  498.6 1.6 fusion.1
  500.2 1.0 concatenate.3
  501.6 46.3 %all-reduce.4 = bf16[16,2048]{1,0:T(8,128)(2,1)S(1)} all-reduce(f32[16,2048]{1,0:T(8,128)S(1)} %fusion.16), channel_id=3, replica_groups=mesh['expert'=8,'dp'=64] {'expert'}, use_global_device_ids=true, to_apply=%region_5.6.clone | all-reduce | flops 32768 | bytes 196608
  (54 shorter events, 8.9 us)
Async XLA Ops:
  7.2 174.4 %copy-start = (bf16[1,2048,128]{2,1,0:T(8,128)(2,1)S(1)}, bf16[1,2048,128]{2,1,0:T(8,128)(2,1)}, u32[]{:S(2)}) copy-start(bf16[1,2048,128]{2,1,0:T(8,128)(2,1)} %param.11) | copy-start | bytes 1572868
  7.2 171.8 %all-gather.7.cloned.1.call-start = ((), (), s32[]{:S(2)}) async-start(), calls=%async_computation.1 | async-start | bytes 2129920 | tf_op jit(solution)/shard_map/all_gather | solution.py:43
  10.3 0.9 copy-start.5
  10.3 0.9 copy-start.6
  10.3 40.5 %copy-start.7 = (bf16[1,2,2048]{2,1,0:T(2,128)(2,1)S(1)}, bf16[1,2,2048]{2,1,0:T(2,128)(2,1)}, u32[]{:S(2)}) copy-start(bf16[1,2,2048]{2,1,0:T(2,128)(2,1)} %param.8) | copy-start | bytes 24580
  50.8 247.1 %all-gather.5.cloned.1.call-start = ((), (), s32[]{:S(2)}) async-start(), calls=%async_computation | async-start | bytes 2129920 | tf_op jit(solution)/shard_map/all_gather | solution.py:49
  181.6 1.0 copy-start.2
  301.6 3.0 copy-start.1
  301.6 3.0 copy-start.8
  305.2 0.7 copy-start.3
  467.7 30.9 %copy-start.4 = (bf16[448,128]{1,0:T(8,128)(2,1)S(1)}, bf16[448,128]{1,0:T(8,128)(2,1)}, u32[]{:S(2)}) copy-start(bf16[448,128]{1,0:T(8,128)(2,1)} %copy-done.3) | copy-start | bytes 344068
  467.7 21.8 %collective-permute-start.6 = (f32[8,2048]{1,0:T(8,128)S(1)}, f32[8,2048]{1,0:T(8,128)S(1)}, u32[]{:S(2)}, u32[]{:S(2)}) collective-permute-start(f32[8,2048]{1,0:T(8,128)S(1)} %fusion), channel_id=1, source_target_pairs={{0,7},{1,8},{2,9},{3,10},{4,11},{5,12},{6,13},{7,14},{8,15},{9,16}... | collective-permute-start | bytes 196616
  469.1 26.9 %collective-permute-start.5 = (f32[8,2048]{1,0:T(8,128)S(1)}, f32[8,2048]{1,0:T(8,128)S(1)}, u32[]{:S(2)}, u32[]{:S(2)}) collective-permute-start(f32[8,2048]{1,0:T(8,128)S(1)} %fusion), channel_id=1, source_target_pairs={{0,6},{1,7},{2,8},{3,9},{4,10},{5,11},{6,12},{7,13},{8,14},{9,15},... | collective-permute-start | bytes 196616
  470.4 17.8 %collective-permute-start.7 = (f32[7,2048]{1,0:T(8,128)S(1)}, f32[7,2048]{1,0:T(8,128)S(1)}, u32[]{:S(2)}, u32[]{:S(2)}) collective-permute-start(f32[7,2048]{1,0:T(8,128)S(1)} %slice.2), channel_id=1, source_target_pairs={{0,8},{1,9},{2,10},{3,11},{4,12},{5,13},{6,14},{7,15},{8,16},{9,17... | collective-permute-start | bytes 172040
  473.3 26.8 %collective-permute-start.4 = (f32[8,2048]{1,0:T(8,128)S(1)}, f32[8,2048]{1,0:T(8,128)S(1)}, u32[]{:S(2)}, u32[]{:S(2)}) collective-permute-start(f32[8,2048]{1,0:T(8,128)S(1)} %fusion), channel_id=1, source_target_pairs={{0,5},{1,6},{2,7},{3,8},{4,9},{5,10},{6,11},{7,12},{8,13},{9,14},{... | collective-permute-start | bytes 196616
  474.6 25.6 %collective-permute-start.3 = (f32[8,2048]{1,0:T(8,128)S(1)}, f32[8,2048]{1,0:T(8,128)S(1)}, u32[]{:S(2)}, u32[]{:S(2)}) collective-permute-start(f32[8,2048]{1,0:T(8,128)S(1)} %fusion), channel_id=1, source_target_pairs={{0,4},{1,5},{2,6},{3,7},{4,8},{5,9},{6,10},{7,11},{8,12},{9,13},{1... | collective-permute-start | bytes 196616
  488.2 12.0 %collective-permute-start.2 = (f32[8,2048]{1,0:T(8,128)S(1)}, f32[8,2048]{1,0:T(8,128)S(1)}, u32[]{:S(2)}, u32[]{:S(2)}) collective-permute-start(f32[8,2048]{1,0:T(8,128)S(1)} %fusion), channel_id=1, source_target_pairs={{0,3},{1,4},{2,5},{3,6},{4,7},{5,8},{6,9},{7,10},{8,11},{9,12},{10... | collective-permute-start | bytes 196616
  489.5 10.7 %collective-permute-start.1 = (f32[8,2048]{1,0:T(8,128)S(1)}, f32[8,2048]{1,0:T(8,128)S(1)}, u32[]{:S(2)}, u32[]{:S(2)}) collective-permute-start(f32[8,2048]{1,0:T(8,128)S(1)} %fusion), channel_id=1, source_target_pairs={{0,2},{1,3},{2,4},{3,5},{4,6},{5,7},{6,8},{7,9},{8,10},{9,11},{10,... | collective-permute-start | bytes 196616
  496.1 4.1 collective-permute-start
Sparse Core Ops, SparseCore 0:
  50.9 128.0 all-gather.6
  181.7 116.1 all-gather.4
where the time goes:
time: 565 us; the launch traced here: 555 us
  blocking collectives  282 us (50%)
  waiting for transfers between devices  200 us (35%)
  starting transfers between devices  29.3 us (5%)
  between operations  15.7 us (3%)
  matrix products  13 us (2%)
  local copies, waits for them, and re-layouts  12.1 us (2%)
    unnamed x2, blocking collectives  206 us
    all_gather x1, waiting for transfers between devices, local(): grad_rows = lax.all_gather(dy_picked, 'dp', axis=0, tiled=True)  115 us
    all_gather x1, waiting for transfers between devices, local(): input_rows = lax.all_gather(x_picked, 'dp', axis=0, tiled=True)  85.8 us
    all_gather x1, blocking collectives, local(): lax.all_gather(tokens, 'expert', axis=1, tiled=True)  38.7 us
    all_gather x1, blocking collectives, local(): lax.all_gather(out_grad, 'expert', axis=1, tiled=True)  37.7 us
    unnamed x8, starting transfers between devices  29.2 us
  transfers between devices with their start and end apart: 10, of which 2 were waited for; matrix products, arithmetic and copies ran while one was open for 2% of the time, Pallas kernels for 0%

commit v1 on v0

v1 whole, which is shorter than its diff:
```python
import jax
import jax.numpy as jnp
from jax import lax
from jax.experimental import pallas as pl
from jax.experimental.pallas import tpu as pltpu
from jax.sharding import PartitionSpec as P

MESH = pl.DeviceIdType.MESH
F32, BF16 = jnp.float32, jnp.bfloat16

NE = 8
NZ = 8
NY = 4
NG = NY * 2
CAP = 7
D = 2048
HD = D // 2
FS = 128
R = NG * CAP
B = 2 * R
CUT = 64
PIECES = ((0, CUT), (CUT, B - CUT))
NT = (((1,), (1,)), ((), ()))


def dot(a, b):
    return jnp.dot(a, b, preferred_element_type=F32)


def dot_nt(a, b):
    return lax.dot_general(a, b, NT, preferred_element_type=F32)


def iota(shape, dim):
    return lax.broadcasted_iota(jnp.int32, shape, dim)


def spread(rows, cols, r_dim):
    r = iota((rows, cols), r_dim)
    c = iota((rows, cols), 1 - r_dim)
    low = jnp.where(r < R, r, r - R)
    group = (low * 37) >> 8
    place = group * 9 + low + jnp.where(r < R, 0, 8)
    return jnp.where(place == c, 1.0, 0.0).astype(BF16)


def kernel(
    tok, cot, ids, scores, wg, wu, wd,
    o_tok, o_gg, o_gu, o_gd,
    gbuf, gf, pick, ybuf, blocks, wall, wdv, wsib, stack, ssib, part, sbuf, rbuf, ysend, yrecv, esend, erecv, gout, gdv,
    load_sem, own_sem, ws_send, ws_recv, g_send, g_recv, y_send, y_recv, sib_send, sib_recv, ag_send, ag_recv,
    ss_send, ss_recv, rs_send, rs_recv, y2_send, y2_recv, e_send, e_recv, out_sem,
):
    e = lax.axis_index("expert")
    d = lax.axis_index("dp")
    z = d // NG
    g = d - z * NG
    h = g % 2
    sib = (e, d + 1 - 2 * h)
    zp = (e, lax.rem(z + 1, NZ) * NG + g)
    zm = (e, lax.rem(z + NZ - 1, NZ) * NG + g)

    def wrap(k):
        return lax.rem(k + 2 * NZ, NZ)

    sent = []

    def send(src, dst, s_sem, r_sem, to):
        copy = pltpu.make_async_remote_copy(
            src_ref=src, dst_ref=dst, send_sem=s_sem, recv_sem=r_sem, device_id=to, device_id_type=MESH
        )
        copy.start()
        sent.append(copy)

    def arrived(dst, r_sem):
        pltpu.make_async_remote_copy(
            src_ref=dst, dst_ref=dst, send_sem=r_sem, recv_sem=r_sem, device_id=sib, device_id_type=MESH
        ).wait_recv()

    loads = [
        pltpu.make_async_copy(tok.at[0], gbuf.at[e, 0], own_sem.at[0]),
        pltpu.make_async_copy(cot.at[0], gbuf.at[e, 1], own_sem.at[1]),
        pltpu.make_async_copy(wd.at[0], wdv, load_sem.at[2]),
        pltpu.make_async_copy(wg.at[0], wall.at[:, 0:FS], load_sem.at[0]),
        pltpu.make_async_copy(wu.at[0], wall.at[:, FS : 2 * FS], load_sem.at[1]),
    ]
    for copy in loads:
        copy.start()

    barrier = pltpu.get_barrier_semaphore()
    for i in range(1, NE):
        pl.semaphore_signal(barrier, inc=1, device_id=(lax.rem(e + i, NE), d), device_id_type=MESH)
    for i in range(1, NG):
        pl.semaphore_signal(barrier, inc=1, device_id=(e, z * NG + lax.rem(g + i, NG)), device_id_type=MESH)
    for to in (zp, zm):
        pl.semaphore_signal(barrier, inc=1, device_id=to, device_id_type=MESH)
    loads[0].wait()
    loads[1].wait()
    pl.semaphore_wait(barrier, NE - 1 + NG - 1 + 2)

    for i in range(1, NE):
        send(gbuf.at[e], gbuf.at[e], g_send.at[i], g_recv.at[e], (lax.rem(e + i, NE), d))
    other = pl.ds(pl.multiple_of((1 - h) * HD, HD), HD)
    send(wg.at[0, other, :], wsib.at[:, 0:FS], ws_send.at[0], ws_recv.at[0], sib)
    send(wu.at[0, other, :], wsib.at[:, FS : 2 * FS], ws_send.at[1], ws_recv.at[1], sib)

    hits = jnp.where(ids[...] == e, 1.0, 0.0)
    named_t = jnp.sum(hits, axis=0, keepdims=True)
    score_t = jnp.sum(hits * scores[...].astype(F32), axis=0, keepdims=True)
    row16, col16 = iota((16, 16), 0), iota((16, 16), 1)
    eye = jnp.where(row16 == col16, 1.0, 0.0)
    named = jnp.sum(eye * named_t, axis=1, keepdims=True)
    slot_t = jnp.sum(jnp.where(row16 < col16, named, 0.0), axis=0, keepdims=True)
    slot = jnp.sum(jnp.where(col16 < row16, named_t, 0.0), axis=1, keepdims=True)
    placing = jnp.where(slot_t == iota((8, 16), 0).astype(F32), named_t, 0.0)
    placing_t = jnp.where(slot == iota((16, 8), 1).astype(F32), named, 0.0)
    weighting = placing * score_t
    zero = jnp.zeros((8, 16), F32)
    picking = jnp.concatenate(
        [jnp.concatenate([placing, zero], axis=1), jnp.concatenate([zero, weighting], axis=1)], axis=0
    ).astype(BF16)

    loads[2].wait()
    wall[:, 2 * FS : 3 * FS] = wdv[...].T

    for i in range(1, NE):
        src = lax.rem(e + i, NE)
        arrived(gbuf.at[src], g_recv.at[src])
    for s in range(NE):
        for a in range(2):
            gf[a * 16 + 2 * s : a * 16 + 2 * s + 2, :] = gbuf[s, a].astype(F32)
    picked = dot(picking, gf[...].astype(BF16)).astype(BF16)
    pick[0] = picked[:, :HD]
    pick[1] = picked[:, HD:]

    for i in range(1, NG):
        to = lax.rem(g + i, NG)
        send(pick.at[to % 2], ybuf.at[g], y_send.at[i], y_recv.at[g], (e, z * NG + to))
    ybuf[g] = pick[h]
    gather = spread(B, NG * 16, 0)
    for i in range(1, NG):
        src = lax.rem(g + i, NG)
        arrived(ybuf.at[src], y_recv.at[src])
    blocks[z, h] = dot(gather, ybuf[...].reshape(NG * 16, HD)).astype(BF16)

    def piece(p):
        return pl.ds(*PIECES[p])

    def ag_start(way, step, p, k):
        ref = blocks.at[k, h, piece(p)]
        send(ref, ref, ag_send.at[way, step, p], ag_recv.at[way, step, p], (zp, zm)[way])

    def ag_wait(way, step, p, k):
        arrived(blocks.at[k, h, piece(p)], ag_recv.at[way, step, p])

    def to_sibling(k):
        ref = blocks.at[k, h]
        send(ref, ref, sib_send.at[k], sib_recv.at[k], sib)

    def fwd(k):
        arrived(blocks.at[k, 1 - h], sib_recv.at[k])
        r = dot(blocks[k, 0], wall[:HD, :]) + dot(blocks[k, 1], wall[HD:, :])
        gate, up, gh = r[:R, :FS], r[:R, FS : 2 * FS], r[R:, 2 * FS :]
        sig = jax.nn.sigmoid(gate)
        act = gate * sig
        none = jnp.zeros((R, FS), F32)
        gate_delta = gh * up * sig * (1.0 + gate * (1.0 - sig))
        stack[k, :, 0:FS] = jnp.concatenate([gate_delta, none], axis=0).astype(BF16)
        stack[k, :, FS : 2 * FS] = jnp.concatenate([gh * act, none], axis=0).astype(BF16)
        stack[k, :, 2 * FS :] = jnp.concatenate([none, act * up], axis=0).astype(BF16)
        send(stack.at[k, 0:CUT, 0 : 2 * FS], ssib.at[k], ss_send.at[k], ss_recv.at[k], sib)

    mine = pl.ds(pl.multiple_of(h * HD, HD), HD)

    def row_grad(k):
        arrived(ssib.at[k], ss_recv.at[k])
        r = dot_nt(stack[k, 0:CUT, 0 : 2 * FS], wall[mine, 0 : 2 * FS]) + dot_nt(ssib[k], wsib[...])
        part[k] = jnp.concatenate([r[:R, : HD // 2], r[:R, HD // 2 :]], axis=0)

    for p in range(2):
        for way in range(2):
            ag_start(way, 0, p, z)
    to_sibling(z)
    for copy in loads[3:]:
        copy.wait()
    for i in range(2):
        arrived(wsib.at[:, i * FS : (i + 1) * FS], ws_recv.at[i])

    def near(way, s):
        return wrap(z - s if way == 0 else z + s)

    def rs_start(way, step, p, value):
        rows = PIECES[p]
        sbuf[way, step, rows[0] : rows[0] + rows[1]] = value.astype(BF16)
        send(
            sbuf.at[way, step, piece(p)], rbuf.at[way, step, piece(p)],
            rs_send.at[way, step, p], rs_recv.at[way, step, p], (zp, zm)[way],
        )

    def rs_take(way, step, p):
        arrived(rbuf.at[way, step, piece(p)], rs_recv.at[way, step, p])
        rows = PIECES[p]
        return rbuf[way, step, rows[0] : rows[0] + rows[1]].astype(F32)

    def part_of(k, p):
        rows = PIECES[p]
        return part[k, rows[0] : rows[0] + rows[1]]

    work = {
        (1, 0): [(fwd, z)],
        (1, 1): [],
        (2, 0): [(fwd, near(0, 1)), (row_grad, z)],
        (2, 1): [(fwd, near(1, 1))],
        (3, 0): [(fwd, near(0, 2)), (row_grad, near(0, 1))],
        (3, 1): [(fwd, near(1, 2)), (row_grad, near(1, 1))],
    }
    for s in range(1, 4):
        for p in range(2):
            for way in range(2):
                ag_wait(way, s - 1, p, near(way, s))
                if s < 3 or p == way:
                    ag_start(way, s, p, near(way, s))
            if p == 1:
                for way in range(2):
                    to_sibling(near(way, s))
            for f, k in work[s, p]:
                f(k)
    far = wrap(z + 4)
    fwd(near(0, 3))
    row_grad(near(0, 2))
    fwd(near(1, 3))
    row_grad(near(1, 2))
    for way in range(2):
        ag_wait(way, 3, way, far)
    to_sibling(far)
    for way in range(2):
        row_grad(near(way, 3))
    for way in range(2):
        rs_start(way, 1, 1 - way, part_of(near(1 - way, 3), 1 - way))
    fwd(far)
    row_grad(far)
    for way in range(2):
        rs_start(way, 0, way, part_of(far, way))

    stack_t = stack[...].reshape(NZ * B, 3 * FS).T

    def weight_grad(n):
        width = D // 4
        at = n % 2 * width
        cols = blocks[:, n // 2, :, at : at + width].reshape(NZ * B, width)
        r = dot(stack_t, cols)
        gdv[:, n * width : (n + 1) * width] = r[2 * FS :].astype(BF16)
        gout[n * width : (n + 1) * width, :] = r[: 2 * FS].T.astype(BF16)

    for j in range(1, 4):
        weight_grad(j - 1)
        for p in range(2):
            for way in range(2):
                if j == 1 and p != way:
                    continue
                rs_start(way, j, p, part_of(near(1 - way, 4 - j), p) + rs_take(way, j - 1, p))
    weight_grad(3)
    outs = [
        pltpu.make_async_copy(gout.at[:, 0:FS], o_gg.at[0], out_sem.at[0]),
        pltpu.make_async_copy(gout.at[:, FS : 2 * FS], o_gu.at[0], out_sem.at[1]),
        pltpu.make_async_copy(gdv, o_gd.at[0], out_sem.at[2]),
    ]
    for copy in outs:
        copy.start()
    plane = jnp.concatenate(
        [part_of(z, p) + rs_take(0, 3, p) + rs_take(1, 3, p) for p in range(2)], axis=0
    ).astype(BF16)

    ysend[...] = dot(spread(NG * 16, B, 1), plane).astype(BF16).reshape(NG, 16, HD // 2)
    for i in range(1, NG):
        to = lax.rem(g + i, NG)
        send(ysend.at[to], yrecv.at[g], y2_send.at[i], y2_recv.at[g], (e, z * NG + to))
    yrecv[g] = ysend[g]
    for i in range(1, NG):
        src = lax.rem(g + i, NG)
        arrived(yrecv.at[src], y2_recv.at[src])
    halves = [sum(yrecv[y * 2 + c].astype(F32) for y in range(NY)) for c in range(2)]
    rows = jnp.concatenate([halves[0][:8], halves[0][8:], halves[1][:8], halves[1][8:]], axis=1)
    total = placing_t[:, 0:1] * rows[0:1]
    for c in range(1, CAP):
        total += placing_t[:, c : c + 1] * rows[c : c + 1]

    for s in range(NE):
        esend[s] = total[2 * s : 2 * s + 2].astype(BF16)
    for i in range(1, NE):
        to = lax.rem(e + i, NE)
        send(esend.at[to], erecv.at[e], e_send.at[i], e_recv.at[e], (to, d))
    erecv[e] = esend[e]
    for i in range(1, NE):
        src = lax.rem(e + i, NE)
        arrived(erecv.at[src], e_recv.at[src])
    o_tok[0] = sum(erecv[s].astype(F32) for s in range(NE)).astype(BF16)
    for copy in outs:
        copy.wait()
    for copy in sent:
        copy.wait_send()


def local(tokens, out_grad, expert_ids, gate_scores, w_gate, w_up, w_down):
    hbm = pl.BlockSpec(memory_space=pl.ANY)
    vmem = pl.BlockSpec(memory_space=pltpu.VMEM)
    dma = pltpu.SemaphoreType.DMA

    def like(x):
        return jax.ShapeDtypeStruct(x.shape, x.dtype)

    return pl.pallas_call(
        kernel,
        out_shape=(like(tokens), like(w_gate), like(w_up), like(w_down)),
        in_specs=[hbm, hbm, vmem, vmem, hbm, hbm, hbm],
        out_specs=(vmem, hbm, hbm, hbm),
        scratch_shapes=[
            pltpu.VMEM((NE, 2, 2, D), BF16),
            pltpu.VMEM((32, D), F32),
            pltpu.VMEM((2, 16, HD), BF16),
            pltpu.VMEM((NG, 16, HD), BF16),
            pltpu.VMEM((NZ, 2, B, HD), BF16),
            pltpu.VMEM((D, 3 * FS), BF16),
            pltpu.VMEM((FS, D), BF16),
            pltpu.VMEM((HD, 2 * FS), BF16),
            pltpu.VMEM((NZ, B, 3 * FS), BF16),
            pltpu.VMEM((NZ, CUT, 2 * FS), BF16),
            pltpu.VMEM((NZ, B, HD // 2), F32),
            pltpu.VMEM((2, 4, B, HD // 2), BF16),
            pltpu.VMEM((2, 4, B, HD // 2), BF16),
            pltpu.VMEM((NG, 16, HD // 2), BF16),
            pltpu.VMEM((NG, 16, HD // 2), BF16),
            pltpu.VMEM((NE, 2, D), BF16),
            pltpu.VMEM((NE, 2, D), BF16),
            pltpu.VMEM((D, 2 * FS), BF16),
            pltpu.VMEM((FS, D), BF16),
            dma((3,)), dma((2,)), dma((2,)), dma((2,)),
            dma((NE,)), dma((NE,)), dma((NG,)), dma((NG,)),
            dma((NZ,)), dma((NZ,)), dma((2, 4, 2)), dma((2, 4, 2)),
            dma((NZ,)), dma((NZ,)), dma((2, 4, 2)), dma((2, 4, 2)),
            dma((NG,)), dma((NG,)), dma((NE,)), dma((NE,)), dma((3,)),
        ],
        compiler_params=pltpu.CompilerParams(
            collective_id=0, has_side_effects=True, vmem_limit_bytes=50 * 2**20
        ),
        cost_estimate=pl.CostEstimate(flops=4 * 10**9, bytes_accessed=4 * 10**6, transcendentals=10**5),
    )(
        tokens, out_grad, jnp.swapaxes(expert_ids[0], 0, 1), jnp.swapaxes(gate_scores[0], 0, 1),
        w_gate, w_up, w_down,
    )


def solution(mesh):
    return jax.shard_map(
        local,
        mesh=mesh,
        in_specs=(
            P("dp", "expert", None),
            P("dp", "expert", None),
            P("dp", None, None),
            P("dp", None, None),
            P("expert", None, "dp"),
            P("expert", None, "dp"),
            P("expert", "dp", None),
        ),
        out_specs=(
            P("dp", "expert", None),
            P("expert", None, "dp"),
            P("expert", None, "dp"),
            P("expert", "dp", None),
        ),
        check_vma=False,
    )
```

time: 565 us -> 90.5 us (0.16); the launches traced: 555 us -> 90.2 us
  blocking collectives: 282 us -> 0 us
  waiting for transfers between devices: 200 us -> 0 us
  Pallas kernels: 0 us -> 81.4 us
  starting transfers between devices: 29.3 us -> 0 us
  between operations: 15.7 us -> 0.66 us
  matrix products: 13 us -> 0 us
    unnamed x2 -> x0, blocking collectives: 206 us -> none
    all_gather x2 -> x0, waiting for transfers between devices: 200 us -> none  [the longest x1 115 us: local(): grad_rows = lax.all_gather(dy_picked, 'dp', axis=0, tiled=True)]
    pallas_call x0 -> x1, Pallas kernels: none -> 81.4 us  [local(): pl.pallas_call(kernel, out_shape=(like(tokens), like(w_gate), like(w_up),...]
    all_gather x2 -> x0, blocking collectives: 76.4 us -> none  [the longest x1 38.7 us: local(): lax.all_gather(tokens, 'expert', axis=1, tiled=True)]
    unnamed x8 -> x0, starting transfers between devices: 29.2 us -> none
    dot_general x11 -> x0, matrix products: 13 us -> none  [the longest x1 2.95 us: local(): jnp.dot(hidden.T, grad_rows, preferred_element_type=jnp.float32)]
  transfers between devices with their start and end apart: 10 -> 0, of which waited for: 2 -> 0; matrix products, arithmetic and copies ran while one was open for 2% -> 0% of each run, Pallas kernels for 0% -> 0%
where the time goes in v1:
time: 90.5 us; the launch traced here: 90.2 us
  Pallas kernels  81.4 us (90%)
  local copies, waits for them, and re-layouts  8.16 us (9%)
    pallas_call x1, Pallas kernels, local(): pl.pallas_call(kernel, out_shape=(like(tokens), like(w_gate), like(w_up),...  81.4 us
    unnamed x18, local copies, waits for them, and re-layouts  8.16 us

profile of v1, /device:TPU:1, one launch (start us, length us, event | category | flops | bytes accessed | tf_op | source)
XLA Modules:
  0.0 90.2 jit_solution(515775233685423952)
XLA Ops:
  0.6 0.0 copy-start.5
  0.6 0.0 copy-start.6
  0.7 0.7 copy-done.5
  1.3 0.0 copy-done.6
  1.3 0.0 copy-start
  1.3 1.0 %copy-done = bf16[1,2048,128]{2,1,0:T(8,128)(2,1)S(1)} copy-done((bf16[1,2048,128]{2,1,0:T(8,128)(2,1)S(1)}, bf16[1,2048,128]{2,1,0:T(8,128)(2,1)}, u32[]{:S(2)}) %copy-start) | copy-done | bytes 524312
  2.4 0.0 copy-start.1
  2.4 1.0 %copy-done.1 = bf16[1,2048,128]{2,1,0:T(8,128)(2,1)S(1)} copy-done((bf16[1,2048,128]{2,1,0:T(8,128)(2,1)S(1)}, bf16[1,2048,128]{2,1,0:T(8,128)(2,1)}, u32[]{:S(2)}) %copy-start.1) | copy-done | bytes 524312
  3.4 0.0 copy-start.2
  3.4 1.0 %copy-done.2 = bf16[1,128,2048]{2,1,0:T(8,128)(2,1)S(1)} copy-done((bf16[1,128,2048]{2,1,0:T(8,128)(2,1)S(1)}, bf16[1,128,2048]{2,1,0:T(8,128)(2,1)}, u32[]{:S(2)}) %copy-start.2) | copy-done | bytes 524312
  4.4 0.0 copy-start.3
  4.4 0.7 copy-done.3
  5.1 0.0 copy-start.4
  5.1 0.7 copy-done.4
  5.8 81.4 %shard_map.102 = (bf16[1,2,2048]{2,1,0:T(2,128)(2,1)S(1)}, bf16[1,2048,128]{2,1,0:T(8,128)(2,1)S(1)}, bf16[1,2048,128]{2,1,0:T(8,128)(2,1)S(1)}, bf16[1,128,2048]{2,1,0:T(8,128)(2,1)S(1)}) custom-call(bf16[1,2,2048]{2,1,0:T(2,128)(2,1)S(1)} %copy-done.3, bf16[1,2,2048]{2,1,0:T(2,128)(2,1)S(1)} %copy-done.4, s32[2,16]{1,0:T(2,128)S(1)} %bitcast.6, ...), custom_call_target="tpu_custom_call" | custom-call | flops 4000000000 | bytes 4000000 | tf_op jit(solution)/shard_map/pallas_call | solution.py:312
  87.2 0.6 copy.15
  87.8 0.8 copy.16
  88.6 0.8 copy.17
  89.4 0.8 copy.18
Async XLA Ops:
  0.6 0.7 copy-start.5
  0.6 0.7 copy-start.6
  1.3 1.0 %copy-start = (bf16[1,2048,128]{2,1,0:T(8,128)(2,1)S(1)}, bf16[1,2048,128]{2,1,0:T(8,128)(2,1)}, u32[]{:S(2)}) copy-start(bf16[1,2048,128]{2,1,0:T(8,128)(2,1)} %wg.1) | copy-start | bytes 1572868
  2.4 1.0 %copy-start.1 = (bf16[1,2048,128]{2,1,0:T(8,128)(2,1)S(1)}, bf16[1,2048,128]{2,1,0:T(8,128)(2,1)}, u32[]{:S(2)}) copy-start(bf16[1,2048,128]{2,1,0:T(8,128)(2,1)} %wu.1) | copy-start | bytes 1572868
  3.4 1.0 %copy-start.2 = (bf16[1,128,2048]{2,1,0:T(8,128)(2,1)S(1)}, bf16[1,128,2048]{2,1,0:T(8,128)(2,1)}, u32[]{:S(2)}) copy-start(bf16[1,128,2048]{2,1,0:T(8,128)(2,1)} %wd.1) | copy-start | bytes 1572868
  4.4 0.7 copy-start.3
  5.1 0.7 copy-start.4

commit v2 on v1

v2 whole, which is shorter than its diff:
```python
import jax
import jax.numpy as jnp
from jax import lax
from jax.experimental import pallas as pl
from jax.experimental.pallas import tpu as pltpu
from jax.sharding import PartitionSpec as P

MESH = pl.DeviceIdType.MESH
F32, BF16 = jnp.float32, jnp.bfloat16

NE = 8
NZ = 8
NY = 4
NG = NY * 2
CAP = 7
D = 2048
HD = D // 2
FS = 128
R = NG * CAP
B = 2 * R
Q = HD // 2
CUT = 64
NA = 1
V = Q // NA
NQ = 4
W = Q // NQ
NT = (((1,), (1,)), ((), ()))


def dot(a, b):
    return jnp.dot(a, b, preferred_element_type=F32)


def dot_nt(a, b):
    return lax.dot_general(a, b, NT, preferred_element_type=F32)


def iota(shape, dim):
    return lax.broadcasted_iota(jnp.int32, shape, dim)


def spread(rows, cols, r_dim):
    r = iota((rows, cols), r_dim)
    c = iota((rows, cols), 1 - r_dim)
    low = jnp.where(r < R, r, r - R)
    group = (low * 37) >> 8
    place = group * 9 + low + jnp.where(r < R, 0, 8)
    return jnp.where(place == c, 1.0, 0.0).astype(BF16)


def kernel(
    tok, cot, ids_in, scores_in, wg, wu, wd,
    o_tok, o_gg, o_gu, o_gd,
    ids, scores, gbuf, gf, pick, ybuf, blocks, wx, wy, wdv, wsib, stack, stack_h, ssib, part, sbuf, rbuf, ysend, yrecv, esend, erecv,
    load_sem, own_sem, ws_send, ws_recv, g_send, g_recv, y_send, y_recv, sib_send, sib_recv, ag_send, ag_recv,
    ss_send, ss_recv, rs_send, rs_recv, y2_send, y2_recv, e_send, e_recv,
):
    e = lax.axis_index("expert")
    d = lax.axis_index("dp")
    z = d // NG
    g = d - z * NG
    h = g % 2
    e_x = e // 2
    e_y = e - 2 * e_x
    across = e + 1 - 2 * e_y
    along = [lax.rem(e_x + i, NE // 2) * 2 + e_y for i in (1, 3, 2)]
    sib = (e, d + 1 - 2 * h)
    zp = (e, lax.rem(z + 1, NZ) * NG + g)
    zm = (e, lax.rem(z + NZ - 1, NZ) * NG + g)

    def wrap(k):
        return lax.rem(k + 2 * NZ, NZ)

    sent = []

    def send(src, dst, s_sem, r_sem, to):
        copy = pltpu.make_async_remote_copy(
            src_ref=src, dst_ref=dst, send_sem=s_sem, recv_sem=r_sem, device_id=to, device_id_type=MESH
        )
        copy.start()
        sent.append(copy)

    def arrived(dst, r_sem):
        pltpu.make_async_remote_copy(
            src_ref=dst, dst_ref=dst, send_sem=r_sem, recv_sem=r_sem, device_id=sib, device_id_type=MESH
        ).wait_recv()

    own = [
        pltpu.make_async_copy(tok.at[0], gbuf.at[e, 0], own_sem.at[0]),
        pltpu.make_async_copy(cot.at[0], gbuf.at[e, 1], own_sem.at[1]),
        pltpu.make_async_copy(ids_in, ids, own_sem.at[2]),
        pltpu.make_async_copy(scores_in, scores, own_sem.at[3]),
    ]
    for copy in own:
        copy.start()
    load_wd = pltpu.make_async_copy(wd.at[0], wdv, load_sem.at[8])
    load_wd.start()
    loads = []
    for n, w in enumerate((wg, wu)):
        for q in range(4):
            at = q % 2 * 2 * FS + n * FS
            loads.append(
                pltpu.make_async_copy(
                    w.at[0, q * Q : (q + 1) * Q, :], wx.at[q // 2, :, at : at + FS], load_sem.at[n * 4 + q]
                )
            )
    for copy in loads:
        copy.start()

    barrier = pltpu.get_barrier_semaphore()
    near_by = [(k, d) for k in (across, *along)]
    near_by += [(e, z * NG + lax.rem(g + i, NG)) for i in range(1, NG)] + [zp, zm]
    for to in near_by:
        pl.semaphore_signal(barrier, inc=1, device_id=to, device_id_type=MESH)
    for copy in own:
        copy.wait()
    pl.semaphore_wait(barrier, len(near_by))

    for a in range(2):
        for i, k in enumerate((across, *along)):
            send(gbuf.at[e, a], gbuf.at[e, a], g_send.at[a, i], g_recv.at[a, e], (k, d))
    for n, w in enumerate((wg, wu)):
        for f in range(2):
            rows = pl.ds(pl.multiple_of((1 - h) * HD + f * Q, Q), Q)
            send(w.at[0, rows, :], wsib.at[f, :, n * FS : (n + 1) * FS], ws_send.at[n, f], ws_recv.at[n, f], sib)

    hits = jnp.where(ids[...] == e, 1.0, 0.0)
    named_t = jnp.sum(hits, axis=0, keepdims=True)
    score_t = jnp.sum(hits * scores[...].astype(F32), axis=0, keepdims=True)
    row16, col16 = iota((16, 16), 0), iota((16, 16), 1)
    eye = jnp.where(row16 == col16, 1.0, 0.0)
    named = jnp.sum(eye * named_t, axis=1, keepdims=True)
    slot_t = jnp.sum(jnp.where(row16 < col16, named, 0.0), axis=0, keepdims=True)
    slot = jnp.sum(jnp.where(col16 < row16, named_t, 0.0), axis=1, keepdims=True)
    placing = jnp.where(slot_t == iota((8, 16), 0).astype(F32), named_t, 0.0)
    placing_t = jnp.where(slot == iota((16, 8), 1).astype(F32), named, 0.0)
    picking = (placing.astype(BF16), (placing * score_t).astype(BF16))
    gather = spread(B, NG * 16, 0)

    load_wd.wait()
    for q in range(4):
        wy[q // 2, :, q % 2 * FS : (q % 2 + 1) * FS] = wdv[:, q * Q : (q + 1) * Q].T

    for a in range(2):
        arrived(gbuf.at[across, a], g_recv.at[a, across])
        for i, k in enumerate(along):
            send(gbuf.at[across, a], gbuf.at[across, a], g_send.at[a, 4 + i], g_recv.at[a, across], (k, d))

    for a in range(2):
        for k in along:
            for src in (k, k + 1 - 2 * e_y):
                arrived(gbuf.at[src, a], g_recv.at[a, src])
        for s in range(NE):
            gf[a, 2 * s : 2 * s + 2, :] = gbuf[s, a].astype(F32)
        picked = dot(picking[a], gf[a].astype(BF16))
        for c in range(2):
            at = c * HD
            pick[a, c] = jnp.concatenate([picked[:, at : at + Q], picked[:, at + Q : at + HD]], axis=0).astype(BF16)
        for i in range(1, NG):
            to = lax.rem(g + i, NG)
            send(pick.at[a, to % 2], ybuf.at[a, g], y_send.at[a, i], y_recv.at[a, g], (e, z * NG + to))
        ybuf[a, g] = pick[a, h]

    def ag_piece(a, k, c, n):
        return blocks.at[a, k, c, :, pl.ds(n * V, V)]

    def ag_start(way, step, a, k, n):
        ref = ag_piece(a, k, h, n)
        send(ref, ref, ag_send.at[way, step, a, n], ag_recv.at[way, step, a, n], (zp, zm)[way])

    def ag_wait(way, step, a, k, n):
        arrived(ag_piece(a, k, h, n), ag_recv.at[way, step, a, n])

    def to_sibling(a, k, n):
        ref = ag_piece(a, k, h, n)
        send(ref, ref, sib_send.at[a, k, n], sib_recv.at[a, k, n], sib)

    def fwd(k):
        for a in range(2):
            for n in range(NA):
                arrived(ag_piece(a, k, 1 - h, n), sib_recv.at[a, k, n])
        r = dot(blocks[0, k, 0], wx[0]) + dot(blocks[0, k, 1], wx[1])
        pre = r[:R, : 2 * FS] + r[R:, 2 * FS :]
        r = dot(blocks[1, k, 0], wy[0]) + dot(blocks[1, k, 1], wy[1])
        gh = r[:R, :FS] + r[R:, FS:]
        gate, up = pre[:, :FS], pre[:, FS:]
        sig = jax.nn.sigmoid(gate)
        act = gate * sig
        none = jnp.zeros((R, FS), F32)
        gate_delta = gh * up * sig * (1.0 + gate * (1.0 - sig))
        for n, delta in enumerate((gate_delta, gh * act)):
            stack[k, :, n * FS : (n + 1) * FS] = jnp.concatenate([delta, none], axis=0).astype(BF16)
            stack[k, :, (n + 2) * FS : (n + 3) * FS] = jnp.concatenate([none, delta], axis=0).astype(BF16)
        hidden = act * up
        stack_h[k, :, :FS] = jnp.concatenate([hidden, none], axis=0).astype(BF16)
        stack_h[k, :, FS:] = jnp.concatenate([none, hidden], axis=0).astype(BF16)
        send(stack.at[k, 0:CUT, 0 : 2 * FS], ssib.at[k], ss_send.at[k], ss_recv.at[k], sib)

    def row_grad(k):
        arrived(ssib.at[k], ss_recv.at[k])
        delta, delta_sib = stack[k, 0:CUT, 0 : 2 * FS], ssib[k]
        part[k] = jnp.concatenate(
            [
                (dot_nt(delta, wx[h, :, f * 2 * FS : (f + 1) * 2 * FS]) + dot_nt(delta_sib, wsib[f]))[:R]
                for f in range(2)
            ],
            axis=0,
        )

    for a in range(2):
        for i in range(1, NG):
            src = lax.rem(g + i, NG)
            arrived(ybuf.at[a, src], y_recv.at[a, src])
        blocks[a, z, h] = dot(gather, ybuf[a].reshape(NG * 16, Q)).astype(BF16)
        for n in range(NA):
            for way in range(2):
                ag_start(way, 0, a, z, n)
        for n in range(NA):
            to_sibling(a, z, n)
    for copy in loads:
        copy.wait()
    for n in range(2):
        for f in range(2):
            arrived(wsib.at[f, :, n * FS : (n + 1) * FS], ws_recv.at[n, f])

    def near(way, s):
        return wrap(z - s if way == 0 else z + s)

    def lanes(q):
        return pl.ds(q * W, W)

    def rs_start(way, step, q, value):
        sbuf[way, step, :, q * W : (q + 1) * W] = value.astype(BF16)
        send(
            sbuf.at[way, step, :, lanes(q)], rbuf.at[way, step, :, lanes(q)],
            rs_send.at[way, step, q], rs_recv.at[way, step, q], (zp, zm)[way],
        )

    def rs_take(way, step, q):
        arrived(rbuf.at[way, step, :, lanes(q)], rs_recv.at[way, step, q])
        return rbuf[way, step, :, q * W : (q + 1) * W].astype(F32)

    def part_of(k, q):
        return part[k, :, q * W : (q + 1) * W]

    work = {
        (1, 0): [(fwd, z)],
        (1, 1): [],
        (2, 0): [(fwd, near(0, 1)), (row_grad, z)],
        (2, 1): [(fwd, near(1, 1))],
        (3, 0): [(fwd, near(0, 2)), (row_grad, near(0, 1))],
        (3, 1): [(fwd, near(1, 2)), (row_grad, near(1, 1))],
    }
    for s in range(1, 4):
        for a in range(2):
            for n in range(NA):
                for way in range(2):
                    ag_wait(way, s - 1, a, near(way, s), n)
                    if s < 3 or a == way:
                        ag_start(way, s, a, near(way, s), n)
                    to_sibling(a, near(way, s), n)
            for f, k in work[s, a]:
                f(k)
    far = wrap(z + 4)
    fwd(near(0, 3))
    row_grad(near(0, 2))
    fwd(near(1, 3))
    row_grad(near(1, 2))
    for n in range(NA):
        for way in range(2):
            ag_wait(way, 3, way, far, n)
            to_sibling(way, far, n)
    for way in range(2):
        row_grad(near(way, 3))

    def first(way, q):
        return (q < NQ // 2) == (way == 0)

    for q in range(NQ):
        for way in range(2):
            if not first(way, q):
                rs_start(way, 1, q, part_of(near(1 - way, 3), q))
    fwd(far)
    row_grad(far)
    for q in range(NQ):
        for way in range(2):
            if first(way, q):
                rs_start(way, 0, q, part_of(far, q))

    def weight_grad(c):
        if c == 0:
            r = dot(stack_t, blocks[0, :, 0].reshape(NZ * B, Q))
        elif c == 1:
            r = dot(stack_t, blocks[0, :, 1].reshape(NZ * B, Q))
        else:
            r = None
        if r is not None:
            for f in range(2):
                at = c * HD + f * Q
                both = r[f * 2 * FS : (f + 1) * 2 * FS].T.astype(BF16)
                o_gg[0, at : at + Q, :] = both[:, :FS]
                o_gu[0, at : at + Q, :] = both[:, FS:]
            return
        stack_ht = stack_h[...].reshape(NZ * B, 2 * FS).T
        for c in range(2):
            r = dot(stack_ht, blocks[1, :, c].reshape(NZ * B, Q))
            for f in range(2):
                at = c * HD + f * Q
                o_gd[0, :, at : at + Q] = r[f * FS : (f + 1) * FS].astype(BF16)

    stack_t = stack[...].reshape(NZ * B, 4 * FS).T
    for j in range(1, 4):
        weight_grad(j - 1)
        for q in range(NQ):
            for way in range(2):
                if j == 1 and not first(way, q):
                    continue
                rs_start(way, j, q, part_of(near(1 - way, 4 - j), q) + rs_take(way, j - 1, q))

    scatter = spread(NG * 16, B, 1)
    for q in range(2):
        plane = jnp.concatenate(
            [
                (part_of(z, p) + rs_take(0, 3, p) + rs_take(1, 3, p)).astype(BF16)
                for p in range(q * NQ // 2, (q + 1) * NQ // 2)
            ],
            axis=1,
        )
        ysend[q] = dot(scatter, plane).astype(BF16).reshape(NG, 16, Q // 2)
        for i in range(1, NG):
            to = lax.rem(g + i, NG)
            send(ysend.at[q, to], yrecv.at[q, g], y2_send.at[q, i], y2_recv.at[q, g], (e, z * NG + to))
        yrecv[q, g] = ysend[q, g]
    quarters = {}
    for q in range(2):
        for i in range(1, NG):
            src = lax.rem(g + i, NG)
            arrived(yrecv.at[q, src], y2_recv.at[q, src])
        for c in range(2):
            r = sum(yrecv[q, y * 2 + c].astype(F32) for y in range(NY))
            for f in range(2):
                quarters[c, f, q] = r[f * 8 : f * 8 + 8]
    rows = jnp.concatenate([quarters[c, f, q] for c in range(2) for f in range(2) for q in range(2)], axis=1)
    total = placing_t[:, 0:1] * rows[0:1]
    for c in range(1, CAP):
        total += placing_t[:, c : c + 1] * rows[c : c + 1]

    for s in range(NE):
        esend[s] = total[2 * s : 2 * s + 2].astype(BF16)
    for i in range(1, NE):
        to = lax.rem(e + i, NE)
        send(esend.at[to], erecv.at[e], e_send.at[i], e_recv.at[e], (to, d))
    erecv[e] = esend[e]
    for i in range(1, NE):
        src = lax.rem(e + i, NE)
        arrived(erecv.at[src], e_recv.at[src])
    o_tok[0] = sum(erecv[s].astype(F32) for s in range(NE)).astype(BF16)
    for copy in sent:
        copy.wait_send()


def write(a0, a1, a2, a3, o0, o1, o2, o3, sems):
    copies = [
        pltpu.make_async_copy(src, dst, sems.at[i])
        for i, (src, dst) in enumerate(((a0, o0), (a1, o1), (a2, o2), (a3, o3)))
    ]
    for copy in copies:
        copy.start()
    for copy in copies:
        copy.wait()


def local(tokens, out_grad, expert_ids, gate_scores, w_gate, w_up, w_down):
    hbm = pl.BlockSpec(memory_space=pl.ANY)
    far = pl.BlockSpec(memory_space=pltpu.HBM)
    vmem = pl.BlockSpec(memory_space=pltpu.VMEM)
    dma = pltpu.SemaphoreType.DMA

    def keep(x):
        return pltpu.with_memory_space_constraint(x, pltpu.HBM)

    def like(x):
        return jax.ShapeDtypeStruct(x.shape, x.dtype)

    shapes = (like(tokens), like(w_gate), like(w_up), like(w_down))
    made = pl.pallas_call(
        kernel,
        out_shape=shapes,
        in_specs=[far] * 7,
        out_specs=(vmem,) * 4,
        scratch_shapes=[
            pltpu.VMEM((2, 16), jnp.int32),
            pltpu.VMEM((2, 16), BF16),
            pltpu.VMEM((NE, 2, 2, D), BF16),
            pltpu.VMEM((2, 16, D), F32),
            pltpu.VMEM((2, 2, 16, Q), BF16),
            pltpu.VMEM((2, NG, 16, Q), BF16),
            pltpu.VMEM((2, NZ, 2, B, Q), BF16),
            pltpu.VMEM((2, Q, 4 * FS), BF16),
            pltpu.VMEM((2, Q, 2 * FS), BF16),
            pltpu.VMEM((FS, D), BF16),
            pltpu.VMEM((2, Q, 2 * FS), BF16),
            pltpu.VMEM((NZ, B, 4 * FS), BF16),
            pltpu.VMEM((NZ, B, 2 * FS), BF16),
            pltpu.VMEM((NZ, CUT, 2 * FS), BF16),
            pltpu.VMEM((NZ, B, Q), F32),
            pltpu.VMEM((2, 4, B, Q), BF16),
            pltpu.VMEM((2, 4, B, Q), BF16),
            pltpu.VMEM((2, NG, 16, Q // 2), BF16),
            pltpu.VMEM((2, NG, 16, Q // 2), BF16),
            pltpu.VMEM((NE, 2, D), BF16),
            pltpu.VMEM((NE, 2, D), BF16),
            dma((9,)), dma((4,)), dma((2, 2)), dma((2, 2)),
            dma((2, 7)), dma((2, NE)), dma((2, NG)), dma((2, NG)),
            dma((2, NZ, NA)), dma((2, NZ, NA)), dma((2, 4, 2, NA)), dma((2, 4, 2, NA)),
            dma((NZ,)), dma((NZ,)), dma((2, 4, NQ)), dma((2, 4, NQ)),
            dma((2, NG)), dma((2, NG)), dma((NE,)), dma((NE,)),
        ],
        compiler_params=pltpu.CompilerParams(
            collective_id=0, has_side_effects=True, vmem_limit_bytes=40 * 2**20
        ),
        cost_estimate=pl.CostEstimate(flops=4 * 10**9, bytes_accessed=4 * 10**6, transcendentals=10**5),
    )(
        keep(tokens), keep(out_grad), keep(jnp.swapaxes(expert_ids[0], 0, 1)), keep(jnp.swapaxes(gate_scores[0], 0, 1)),
        keep(w_gate), keep(w_up), keep(w_down),
    )
    return pl.pallas_call(
        write,
        out_shape=shapes,
        in_specs=[vmem] * 4,
        out_specs=(far,) * 4,
        scratch_shapes=[dma((4,))],
        compiler_params=pltpu.CompilerParams(vmem_limit_bytes=16 * 2**20),
    )(*made)


def solution(mesh):
    return jax.shard_map(
        local,
        mesh=mesh,
        in_specs=(
            P("dp", "expert", None),
            P("dp", "expert", None),
            P("dp", None, None),
            P("dp", None, None),
            P("expert", None, "dp"),
            P("expert", None, "dp"),
            P("expert", "dp", None),
        ),
        out_specs=(
            P("dp", "expert", None),
            P("expert", None, "dp"),
            P("expert", None, "dp"),
            P("expert", "dp", None),
        ),
        check_vma=False,
    )
```

time: 90.5 us -> 81.3 us (0.90)
  local copies, waits for them, and re-layouts: 8.16 us -> 0 us
    unnamed x18 -> x0, local copies, waits for them, and re-layouts: 8.16 us -> none
    pallas_call x1 -> x2, Pallas kernels: 81.4 us -> 80.5 us  [the longest x1 79.3 us: local(): pl.pallas_call(kernel, out_shape=shapes, in_specs=[far] * 7, out_specs=(v...]
where the time goes in v2:
time: 81.3 us; the launch traced here: 81.1 us
  Pallas kernels  80.5 us (99%)
    pallas_call x1, Pallas kernels, local(): pl.pallas_call(kernel, out_shape=shapes, in_specs=[far] * 7, out_specs=(v...  79.3 us

profile of v2, /device:TPU:1, one launch (start us, length us, event | category | flops | bytes accessed | tf_op | source)
XLA Modules:
  0.0 81.1 jit_solution(918159541654421271)
XLA Ops:
  0.6 79.3 %shard_map.102 = (bf16[1,2,2048]{2,1,0:T(2,128)(2,1)S(1)}, bf16[1,2048,128]{2,1,0:T(8,128)(2,1)S(1)}, bf16[1,2048,128]{2,1,0:T(8,128)(2,1)S(1)}, bf16[1,128,2048]{2,1,0:T(8,128)(2,1)S(1)}) custom-call(bf16[1,2,2048]{2,1,0:T(2,128)(2,1)} %tok.1, bf16[1,2,2048]{2,1,0:T(2,128)(2,1)} %cot.1, s32[2,16]{1,0:T(2,128)} %bitcast.6, bf16[2,16]{1,0:T(2,128)(2,1)} %bitcast.7, ...), custom_call_target="tpu_custom_call" | custom-call | flops 4000000000 | bytes 4000000 | tf_op jit(solution)/shard_map/pallas_call | solution.py:386
  80.0 1.2 %shard_map.103 = (bf16[1,2,2048]{2,1,0:T(2,128)(2,1)}, bf16[1,2048,128]{2,1,0:T(8,128)(2,1)}, bf16[1,2048,128]{2,1,0:T(8,128)(2,1)}, bf16[1,128,2048]{2,1,0:T(8,128)(2,1)}) custom-call(bf16[1,2,2048]{2,1,0:T(2,128)(2,1)S(1)} %get-tuple-element.8.a0, bf16[1,2048,128]{2,1,0:T(8,128)(2,1)S(1)} %get-tuple-element.9.a1, ...), custom_call_target="tpu_custom_call" | custom-call | tf_op jit(solution)/shard_map/pallas_call | solution.py:427

commit v3 on v2

--- a/solution.py
+++ b/solution.py
@@ -20,7 +20,7 @@
 B = 2 * R
 Q = HD // 2
 CUT = 64
-NA = 1
+NA = 2
 V = Q // NA
 NQ = 4
 W = Q // NQ
@@ -155,11 +155,17 @@
         picked = dot(picking[a], gf[a].astype(BF16))
         for c in range(2):
             at = c * HD
-            pick[a, c] = jnp.concatenate([picked[:, at : at + Q], picked[:, at + Q : at + HD]], axis=0).astype(BF16)
-        for i in range(1, NG):
-            to = lax.rem(g + i, NG)
-            send(pick.at[a, to % 2], ybuf.at[a, g], y_send.at[a, i], y_recv.at[a, g], (e, z * NG + to))
-        ybuf[a, g] = pick[a, h]
+            both = jnp.concatenate([picked[:, at : at + Q], picked[:, at + Q : at + HD]], axis=0).astype(BF16)
+            for n in range(NA):
+                pick[a, n, c] = both[:, n * V : (n + 1) * V]
+        for n in range(NA):
+            for i in range(1, NG):
+                to = lax.rem(g + i, NG)
+                send(
+                    pick.at[a, n, to % 2], ybuf.at[a, n, g], y_send.at[a, n, i], y_recv.at[a, n, g],
+                    (e, z * NG + to),
+                )
+            ybuf[a, n, g] = pick[a, n, h]
 
     def ag_piece(a, k, c, n):
         return blocks.at[a, k, c, :, pl.ds(n * V, V)]
@@ -208,14 +214,13 @@
         )
 
     for a in range(2):
-        for i in range(1, NG):
-            src = lax.rem(g + i, NG)
-            arrived(ybuf.at[a, src], y_recv.at[a, src])
-        blocks[a, z, h] = dot(gather, ybuf[a].reshape(NG * 16, Q)).astype(BF16)
         for n in range(NA):
+            for i in range(1, NG):
+                src = lax.rem(g + i, NG)
+                arrived(ybuf.at[a, n, src], y_recv.at[a, n, src])
+            blocks[a, z, h, :, n * V : (n + 1) * V] = dot(gather, ybuf[a, n].reshape(NG * 16, V)).astype(BF16)
             for way in range(2):
                 ag_start(way, 0, a, z, n)
-        for n in range(NA):
             to_sibling(a, z, n)
     for copy in loads:
         copy.wait()
@@ -274,7 +279,7 @@
         row_grad(near(way, 3))
 
     def first(way, q):
-        return (q < NQ // 2) == (way == 0)
+        return q % 2 == way
 
     for q in range(NQ):
         for way in range(2):
@@ -331,31 +336,36 @@
             to = lax.rem(g + i, NG)
             send(ysend.at[q, to], yrecv.at[q, g], y2_send.at[q, i], y2_recv.at[q, g], (e, z * NG + to))
         yrecv[q, g] = ysend[q, g]
-    quarters = {}
+    early = len(sent)
     for q in range(2):
         for i in range(1, NG):
             src = lax.rem(g + i, NG)
             arrived(yrecv.at[q, src], y2_recv.at[q, src])
+        rows = []
         for c in range(2):
             r = sum(yrecv[q, y * 2 + c].astype(F32) for y in range(NY))
-            for f in range(2):
-                quarters[c, f, q] = r[f * 8 : f * 8 + 8]
-    rows = jnp.concatenate([quarters[c, f, q] for c in range(2) for f in range(2) for q in range(2)], axis=1)
-    total = placing_t[:, 0:1] * rows[0:1]
-    for c in range(1, CAP):
-        total += placing_t[:, c : c + 1] * rows[c : c + 1]
-
-    for s in range(NE):
-        esend[s] = total[2 * s : 2 * s + 2].astype(BF16)
-    for i in range(1, NE):
-        to = lax.rem(e + i, NE)
-        send(esend.at[to], erecv.at[e], e_send.at[i], e_recv.at[e], (to, d))
-    erecv[e] = esend[e]
-    for i in range(1, NE):
-        src = lax.rem(e + i, NE)
-        arrived(erecv.at[src], e_recv.at[src])
-    o_tok[0] = sum(erecv[s].astype(F32) for s in range(NE)).astype(BF16)
-    for copy in sent:
+            rows += [r[:8], r[8:]]
+        rows = jnp.concatenate(rows, axis=1)
+        total = placing_t[:, 0:1] * rows[0:1]
+        for c in range(1, CAP):
+            total += placing_t[:, c : c + 1] * rows[c : c + 1]
+        for s in range(NE):
+            esend[q, s] = total[2 * s : 2 * s + 2].astype(BF16)
+        for i in range(1, NE):
+            to = lax.rem(e + i, NE)
+            send(esend.at[q, to], erecv.at[q, e], e_send.at[q, i], e_recv.at[q, e], (to, d))
+        erecv[q, e] = esend[q, e]
+    for copy in sent[:early]:
+        copy.wait_send()
+    for q in range(2):
+        for i in range(1, NE):
+            src = lax.rem(e + i, NE)
+            arrived(erecv.at[q, src], e_recv.at[q, src])
+        token = sum(erecv[q, s].astype(F32) for s in range(NE)).astype(BF16)
+        for n in range(4):
+            at = n * Q + q * (Q // 2)
+            o_tok[0, :, at : at + Q // 2] = token[:, n * (Q // 2) : (n + 1) * (Q // 2)]
+    for copy in sent[early:]:
         copy.wait_send()
 
 
@@ -393,8 +403,8 @@
             pltpu.VMEM((2, 16), BF16),
             pltpu.VMEM((NE, 2, 2, D), BF16),
             pltpu.VMEM((2, 16, D), F32),
-            pltpu.VMEM((2, 2, 16, Q), BF16),
-            pltpu.VMEM((2, NG, 16, Q), BF16),
+            pltpu.VMEM((2, NA, 2, 16, V), BF16),
+            pltpu.VMEM((2, NA, NG, 16, V), BF16),
             pltpu.VMEM((2, NZ, 2, B, Q), BF16),
             pltpu.VMEM((2, Q, 4 * FS), BF16),
             pltpu.VMEM((2, Q, 2 * FS), BF16),
@@ -408,13 +418,13 @@
             pltpu.VMEM((2, 4, B, Q), BF16),
             pltpu.VMEM((2, NG, 16, Q // 2), BF16),
             pltpu.VMEM((2, NG, 16, Q // 2), BF16),
-            pltpu.VMEM((NE, 2, D), BF16),
-            pltpu.VMEM((NE, 2, D), BF16),
+            pltpu.VMEM((2, NE, 2, HD), BF16),
+            pltpu.VMEM((2, NE, 2, HD), BF16),
             dma((9,)), dma((4,)), dma((2, 2)), dma((2, 2)),
-            dma((2, 7)), dma((2, NE)), dma((2, NG)), dma((2, NG)),
+            dma((2, 7)), dma((2, NE)), dma((2, NA, NG)), dma((2, NA, NG)),
             dma((2, NZ, NA)), dma((2, NZ, NA)), dma((2, 4, 2, NA)), dma((2, 4, 2, NA)),
             dma((NZ,)), dma((NZ,)), dma((2, 4, NQ)), dma((2, 4, NQ)),
-            dma((2, NG)), dma((2, NG)), dma((NE,)), dma((NE,)),
+            dma((2, NG)), dma((2, NG)), dma((2, NE)), dma((2, NE)),
         ],
         compiler_params=pltpu.CompilerParams(
             collective_id=0, has_side_effects=True, vmem_limit_bytes=40 * 2**20

time: 81.3 us -> 80.7 us (level)
  no operation moved by 1% of the time
where the time goes in v3:
time: 80.7 us; the launch traced here: 80.6 us
  Pallas kernels  79.9 us (99%)
    pallas_call x1, Pallas kernels, local(): pl.pallas_call(kernel, out_shape=shapes, in_specs=[far] * 7, out_specs=(v...  78.7 us

profile of v3, /device:TPU:1, one launch (start us, length us, event | category | flops | bytes accessed | tf_op | source)
XLA Modules:
  0.0 80.6 jit_solution(16787780141303404302)
XLA Ops:
  0.6 78.7 %shard_map.102 = (bf16[1,2,2048]{2,1,0:T(2,128)(2,1)S(1)}, bf16[1,2048,128]{2,1,0:T(8,128)(2,1)S(1)}, bf16[1,2048,128]{2,1,0:T(8,128)(2,1)S(1)}, bf16[1,128,2048]{2,1,0:T(8,128)(2,1)S(1)}) custom-call(bf16[1,2,2048]{2,1,0:T(2,128)(2,1)} %tok.1, bf16[1,2,2048]{2,1,0:T(2,128)(2,1)} %cot.1, s32[2,16]{1,0:T(2,128)} %bitcast.6, bf16[2,16]{1,0:T(2,128)(2,1)} %bitcast.7, ...), custom_call_target="tpu_custom_call" | custom-call | flops 4000000000 | bytes 4000000 | tf_op jit(solution)/shard_map/pallas_call | solution.py:396
  79.4 1.2 %shard_map.103 = (bf16[1,2,2048]{2,1,0:T(2,128)(2,1)}, bf16[1,2048,128]{2,1,0:T(8,128)(2,1)}, bf16[1,2048,128]{2,1,0:T(8,128)(2,1)}, bf16[1,128,2048]{2,1,0:T(8,128)(2,1)}) custom-call(bf16[1,2,2048]{2,1,0:T(2,128)(2,1)S(1)} %get-tuple-element.8.a0, bf16[1,2048,128]{2,1,0:T(8,128)(2,1)S(1)} %get-tuple-element.9.a1, ...), custom_call_target="tpu_custom_call" | custom-call | tf_op jit(solution)/shard_map/pallas_call | solution.py:437

commit v4 on v3

--- a/solution.py
+++ b/solution.py
@@ -84,6 +84,12 @@
         pltpu.make_async_remote_copy(
             src_ref=dst, dst_ref=dst, send_sem=r_sem, recv_sem=r_sem, device_id=sib, device_id_type=MESH
         ).wait_recv()
+
+    barrier = pltpu.get_barrier_semaphore()
+    near_by = [(k, d) for k in (across, *along)]
+    near_by += [(e, z * NG + lax.rem(g + i, NG)) for i in range(1, NG)] + [zp, zm]
+    for to in near_by:
+        pl.semaphore_signal(barrier, inc=1, device_id=to, device_id_type=MESH)
 
     own = [
         pltpu.make_async_copy(tok.at[0], gbuf.at[e, 0], own_sem.at[0]),
@@ -107,11 +113,6 @@
     for copy in loads:
         copy.start()
 
-    barrier = pltpu.get_barrier_semaphore()
-    near_by = [(k, d) for k in (across, *along)]
-    near_by += [(e, z * NG + lax.rem(g + i, NG)) for i in range(1, NG)] + [zp, zm]
-    for to in near_by:
-        pl.semaphore_signal(barrier, inc=1, device_id=to, device_id_type=MESH)
     for copy in own:
         copy.wait()
     pl.semaphore_wait(barrier, len(near_by))
@@ -268,9 +269,7 @@
                 f(k)
     far = wrap(z + 4)
     fwd(near(0, 3))
-    row_grad(near(0, 2))
     fwd(near(1, 3))
-    row_grad(near(1, 2))
     for n in range(NA):
         for way in range(2):
             ag_wait(way, 3, way, far, n)
@@ -286,6 +285,8 @@
             if not first(way, q):
                 rs_start(way, 1, q, part_of(near(1 - way, 3), q))
     fwd(far)
+    row_grad(near(0, 2))
+    row_grad(near(1, 2))
     row_grad(far)
     for q in range(NQ):
         for way in range(2):

time: 80.7 us -> 80.4 us (level)
  no operation moved by 1% of the time
where the time goes in v4:
time: 80.4 us; the launch traced here: 80.3 us
  Pallas kernels  79.6 us (99%)
    pallas_call x1, Pallas kernels, local(): pl.pallas_call(kernel, out_shape=shapes, in_specs=[far] * 7, out_specs=(v...  78.5 us

profile of v4, /device:TPU:1, one launch (start us, length us, event | category | flops | bytes accessed | tf_op | source)
XLA Modules:
  0.0 80.3 jit_solution(5021736254012858143)
XLA Ops:
  0.6 78.5 %shard_map.102 = (bf16[1,2,2048]{2,1,0:T(2,128)(2,1)S(1)}, bf16[1,2048,128]{2,1,0:T(8,128)(2,1)S(1)}, bf16[1,2048,128]{2,1,0:T(8,128)(2,1)S(1)}, bf16[1,128,2048]{2,1,0:T(8,128)(2,1)S(1)}) custom-call(bf16[1,2,2048]{2,1,0:T(2,128)(2,1)} %tok.1, bf16[1,2,2048]{2,1,0:T(2,128)(2,1)} %cot.1, s32[2,16]{1,0:T(2,128)} %bitcast.6, bf16[2,16]{1,0:T(2,128)(2,1)} %bitcast.7, ...), custom_call_target="tpu_custom_call" | custom-call | flops 4000000000 | bytes 4000000 | tf_op jit(solution)/shard_map/pallas_call | solution.py:397
  79.1 1.2 %shard_map.103 = (bf16[1,2,2048]{2,1,0:T(2,128)(2,1)}, bf16[1,2048,128]{2,1,0:T(8,128)(2,1)}, bf16[1,2048,128]{2,1,0:T(8,128)(2,1)}, bf16[1,128,2048]{2,1,0:T(8,128)(2,1)}) custom-call(bf16[1,2,2048]{2,1,0:T(2,128)(2,1)S(1)} %get-tuple-element.8.a0, bf16[1,2048,128]{2,1,0:T(8,128)(2,1)S(1)} %get-tuple-element.9.a1, ...), custom_call_target="tpu_custom_call" | custom-call | tf_op jit(solution)/shard_map/pallas_call | solution.py:438

commit v5 on v4

--- a/solution.py
+++ b/solution.py
@@ -86,7 +86,8 @@
         ).wait_recv()
 
     barrier = pltpu.get_barrier_semaphore()
-    near_by = [(k, d) for k in (across, *along)]
+    beyond = [k + 1 - 2 * e_y for k in along]
+    near_by = [(k, d) for k in (across, *beyond, *along)]
     near_by += [(e, z * NG + lax.rem(g + i, NG)) for i in range(1, NG)] + [zp, zm]
     for to in near_by:
         pl.semaphore_signal(barrier, inc=1, device_id=to, device_id_type=MESH)
@@ -117,8 +118,8 @@
         copy.wait()
     pl.semaphore_wait(barrier, len(near_by))
 
-    for a in range(2):
-        for i, k in enumerate((across, *along)):
+    for a, peers in enumerate(((*beyond, across, *along), (across, *along))):
+        for i, k in enumerate(peers):
             send(gbuf.at[e, a], gbuf.at[e, a], g_send.at[a, i], g_recv.at[a, e], (k, d))
     for n, w in enumerate((wg, wu)):
         for f in range(2):
@@ -142,10 +143,10 @@
     for q in range(4):
         wy[q // 2, :, q % 2 * FS : (q % 2 + 1) * FS] = wdv[:, q * Q : (q + 1) * Q].T
 
-    for a in range(2):
-        arrived(gbuf.at[across, a], g_recv.at[a, across])
-        for i, k in enumerate(along):
-            send(gbuf.at[across, a], gbuf.at[across, a], g_send.at[a, 4 + i], g_recv.at[a, across], (k, d))
+    arrived(gbuf.at[across, 0], g_recv.at[0, across])
+    arrived(gbuf.at[across, 1], g_recv.at[1, across])
+    for i, k in enumerate(along):
+        send(gbuf.at[across, 1], gbuf.at[across, 1], g_send.at[1, 4 + i], g_recv.at[1, across], (k, d))
 
     for a in range(2):
         for k in along:

time: 80.4 us -> 80.4 us (level)
  no operation moved by 1% of the time
where the time goes in v5:
time: 80.4 us; the launch traced here: 80.2 us
  Pallas kernels  79.6 us (99%)
    pallas_call x1, Pallas kernels, local(): pl.pallas_call(kernel, out_shape=shapes, in_specs=[far] * 7, out_specs=(v...  78.4 us

profile of v5, /device:TPU:1, one launch (start us, length us, event | category | flops | bytes accessed | tf_op | source)
XLA Modules:
  0.0 80.2 jit_solution(16430476014346296858)
XLA Ops:
  0.6 78.4 %shard_map.102 = (bf16[1,2,2048]{2,1,0:T(2,128)(2,1)S(1)}, bf16[1,2048,128]{2,1,0:T(8,128)(2,1)S(1)}, bf16[1,2048,128]{2,1,0:T(8,128)(2,1)S(1)}, bf16[1,128,2048]{2,1,0:T(8,128)(2,1)S(1)}) custom-call(bf16[1,2,2048]{2,1,0:T(2,128)(2,1)} %tok.1, bf16[1,2,2048]{2,1,0:T(2,128)(2,1)} %cot.1, s32[2,16]{1,0:T(2,128)} %bitcast.6, bf16[2,16]{1,0:T(2,128)(2,1)} %bitcast.7, ...), custom_call_target="tpu_custom_call" | custom-call | flops 4000000000 | bytes 4000000 | tf_op jit(solution)/shard_map/pallas_call | solution.py:398
  79.1 1.2 %shard_map.103 = (bf16[1,2,2048]{2,1,0:T(2,128)(2,1)}, bf16[1,2048,128]{2,1,0:T(8,128)(2,1)}, bf16[1,2048,128]{2,1,0:T(8,128)(2,1)}, bf16[1,128,2048]{2,1,0:T(8,128)(2,1)}) custom-call(bf16[1,2,2048]{2,1,0:T(2,128)(2,1)S(1)} %get-tuple-element.8.a0, bf16[1,2048,128]{2,1,0:T(8,128)(2,1)S(1)} %get-tuple-element.9.a1, ...), custom_call_target="tpu_custom_call" | custom-call | tf_op jit(solution)/shard_map/pallas_call | solution.py:439
